TPU v7x, 32 devices: a whole 2x2x4 slice. The times are simulated.
32 devices in a mesh: members: 2 (over y), lon: 8 (over z, x), lat: 2 (over core).
Axes of the slice: x: 2, y: 2, z: 4, core: 2. Of those that a mesh axis runs over, the one named last changes fastest.
Arguments:
- field: bfloat16 [256, 88, 384], P(('members', 'lat'), 'lon'), parts along dimension 0, may hold values from -6 to 6
- reach: int32 [128], P('lat'), may hold values from 1 to 2, as said below
- slot_rows: int32 [128, 16], P('lat'), may hold values from 0 to 6
- slot_cols: int32 [128, 16], P('lat'), may hold values from 0 to 3, as said below
- counts: int32 [128], P('lat'), may hold values from 4 to 16, as said below
- filters: bfloat16 [128, 16, 36], P('lat'), may hold values from -1 to 1
- mixing: bfloat16 [3456, 384], replicated, may hold values from -0.109375 to 0.109375
- bias: float32 [384], replicated, may hold values from -3 to 3
Outputs:
- activated: bfloat16 [256, 88, 384], P(('members', 'lat'), 'lon'), parts along dimension 0
There are 2 independent parts, one for each index of `members`. A program takes and returns all parts, laid end to end along the dimension named above; an argument that names none is the same for every part. Nothing has to cross between parts.
Inputs may be any that keep to these rules, and one draw needn't show every extreme that they name: `reach`: the first row reaches 2 blocks. slot_cols[i, s] < 2 reach[i]; the live slots of a row name distinct pairs (slot_rows, slot_cols). `counts`: the first row has 16 live slots.
All inputs are finite; a program needn't handle non-finite values.
Results may differ from a plain program's by a relative error of at most 0.0047.
Values may be sent and summed in bfloat16 or wider, within the bound.
A program may use at most 64 MiB of HBM per device.

v0:
```python
import jax
import jax.numpy as jnp
from jax import lax
from jax.sharding import PartitionSpec as P

BASIS = 9
RAD = 3
BLOCK = 4
SLOTS = 16
HALO = 8


def padded(array, sides, width, wrap):
    for axis, dim in sides:
        size, length = (lax.axis_size(axis), array.shape[dim])
        up = [(i, (i + 1) % size) for i in range(size if wrap else size - 1)]
        down = [(j, i) for i, j in up]
        last = lax.slice_in_dim(array, length - width, length, axis=dim)
        leading = lax.slice_in_dim(array, 0, width, axis=dim)
        before = lax.ppermute(last, axis, up)
        after = lax.ppermute(leading, axis, down)
        array = jnp.concatenate([before, array, after], axis=dim)
    return array


def body(field, reach, slot_rows, slot_cols, counts, filters, mixing, bias):
    rows, cols, width = field.shape
    window_rows = 2 * RAD + 1
    banded = padded(field, (("lat", 0),), RAD, False)
    extended = padded(banded, (("lon", 1),), HALO, True)
    ext_cols = cols + 2 * HALO
    live = (jnp.arange(SLOTS)[None, :] < counts[:, None]).astype(jnp.bfloat16)
    row_hot = (slot_rows[:, :, None] == jnp.arange(window_rows)[None, None, :]).astype(jnp.bfloat16)
    row_hot = row_hot * live[:, :, None]
    starts = (slot_cols - reach[:, None]) * BLOCK + HALO
    shifted = starts[:, :, None, None] + jnp.arange(BLOCK)[None, None, :, None]
    shift_hot = (shifted == jnp.arange(2 * HALO)[None, None, None, :]).astype(jnp.bfloat16)
    slot_taps = filters.reshape(rows, SLOTS, BASIS, BLOCK)
    placed = row_hot[:, :, :, None, None] * slot_taps[:, :, None, :, :]
    profile = jnp.einsum(
        "rsqkt,rstd->rqkd", placed, shift_hot, preferred_element_type=jnp.float32
    ).astype(jnp.bfloat16)
    distance = jnp.arange(ext_cols)[None, :, None] - jnp.arange(cols)[:, None, None]
    band_hot = (distance == jnp.arange(2 * HALO)[None, None, :]).astype(jnp.bfloat16)
    block_rows = 16

    def one_block(block_index):
        first = block_index * block_rows
        block_profile = lax.dynamic_slice_in_dim(profile, first, block_rows, 0)
        band = jnp.einsum(
            "rqkd,lmd->qrlkm", block_profile, band_hot, preferred_element_type=jnp.float32
        )
        band = band.astype(jnp.bfloat16).reshape(window_rows, block_rows, cols * BASIS, ext_cols)
        conv_sum = jnp.zeros((block_rows, cols * BASIS, width), jnp.float32)
        for offset_row in range(window_rows):
            source = lax.dynamic_slice_in_dim(extended, first + offset_row, block_rows, 0)
            conv_sum = conv_sum + jnp.einsum(
                "rxm,rmc->rxc", band[offset_row], source, preferred_element_type=jnp.float32
            )
        conv = conv_sum.astype(jnp.bfloat16).reshape(block_rows * cols, BASIS * width)
        pre_act = jnp.dot(conv, mixing, preferred_element_type=jnp.float32) + bias
        return (
            jax.nn.gelu(pre_act, approximate=False)
            .astype(jnp.bfloat16)
            .reshape(block_rows, cols, width)
        )

    results = lax.map(one_block, jnp.arange(rows // block_rows, dtype=jnp.int32))
    return results.reshape(rows, cols, width)


def solution(mesh):
    return jax.shard_map(
        body,
        mesh=mesh,
        in_specs=(
            P(("members", "lat"), "lon", None),
            P("lat"),
            P("lat", None),
            P("lat", None),
            P("lat"),
            P("lat", None, None),
            P(),
            P(),
        ),
        out_specs=P(("members", "lat"), "lon", None),
        check_vma=False,
    )
```

profile of v0, /device:TPU:1, one launch (start us, length us, event | category | flops | bytes accessed | tf_op | source)
XLA Modules:
  0.0 178.6 jit_solution(1344317533760335507)
XLA Ops:
  2.3 3.0 %collective-permute-start.1 = (bf16[3,11,384]{2,1,0:T(8,128)(2,1)S(1)}, bf16[3,11,384]{2,1,0:T(8,128)(2,1)S(1)}, u32[]{:S(2)}, u32[]{:S(2)}) collective-permute-start(bf16[3,11,384]{2,1,0:T(8,128)(2,1)S(1)} %copy.62), channel_id=1, source_target_pairs={{1,0},{3,2},{5,4},{7,6},{9,8},{11,10},{13,12},{15,14},{17,16},{19,... | collective-permute-start | bytes 76040 | tf_op jit(solution)/shard_map/ppermute | solution.py:21
  7.7 2.5 %copy.32 = bf16[64,16,9,4]{1,2,3,0:T(8,128)(2,1)S(1)} copy(bf16[64,16,9,4]{0,1,3,2:T(8,128)(2,1)} %bitcast.67) | data formatting | bytes 147456 | tf_op jit(solution)/shard_map/mul | solution.py:39
  12.6 2.0 %collective-permute-start.2 = (bf16[70,8,384]{2,1,0:T(8,128)(2,1)}, bf16[70,8,384]{2,1,0:T(8,128)(2,1)S(1)}, u32[]{:S(2)}, u32[]{:S(2)}) collective-permute-start(bf16[70,8,384]{2,1,0:T(8,128)(2,1)} %get-tuple-element.170), channel_id=1, source_target_pairs={{0,2},{2,4},{4,6},{6,8},{8,10},{10,12},{12,14},{14,0},{1,3},{3,5},... | collective-permute-start | bytes 1290248 | tf_op jit(solution)/shard_map/ppermute | solution.py:20
  14.7 3.0 %collective-permute-start.3 = (bf16[70,8,384]{2,1,0:T(8,128)(2,1)S(1)}, bf16[70,8,384]{2,1,0:T(8,128)(2,1)S(1)}, u32[]{:S(2)}, u32[]{:S(2)}) collective-permute-start(bf16[70,8,384]{2,1,0:T(8,128)(2,1)S(1)} %get-tuple-element.171), channel_id=1, source_target_pairs={{2,0},{4,2},{6,4},{8,6},{10,8},{12,10},{14,12},{0,14},{3,1},{5,3},... | collective-permute-start | bytes 1290248 | tf_op jit(solution)/shard_map/ppermute | solution.py:21
  17.7 2.7 %bitcast_convert_fusion = bf16[64,7,9,16]{3,2,1,0:T(8,128)(2,1)S(1)} fusion(bf16[64,16,9,4]{1,2,3,0:T(8,128)(2,1)S(1)} %copy.32, bf16[64,16,7]{1,2,0:T(8,128)(2,1)S(1)} %fusion.57, s32[64,16,4]{1,2,0:T(4,128)S(1)} %iota_add_fusion), kind=kOutput, calls=%fused_computation.60 | convolution fusion | flops 8645632 | bytes 233472 | tf_op jit(solution)/shard_map/rsqkt,rstd->rqkd/dot_general | solution.py:40
  21.7 12.1 %collective-permute-done.2 = bf16[70,8,384]{2,1,0:T(8,128)(2,1)S(1)} collective-permute-done((bf16[70,8,384]{2,1,0:T(8,128)(2,1)}, bf16[70,8,384]{2,1,0:T(8,128)(2,1)S(1)}, u32[]{:S(2)}, u32[]{:S(2)}) %collective-permute-start.2) | collective-permute-done | bytes 430112 | tf_op jit(solution)/shard_map/ppermute | solution.py:20
  33.8 1.9 %collective-permute-done.3 = bf16[70,8,384]{2,1,0:T(8,128)(2,1)S(1)} collective-permute-done((bf16[70,8,384]{2,1,0:T(8,128)(2,1)S(1)}, bf16[70,8,384]{2,1,0:T(8,128)(2,1)S(1)}, u32[]{:S(2)}, u32[]{:S(2)}) %collective-permute-start.3) | collective-permute-done | bytes 430112 | tf_op jit(solution)/shard_map/ppermute | solution.py:21
  37.3 141.3 %while.13 = (s32[]{:T(128)}, bf16[4,16,11,384]{3,1,0,2:T(8,128)(2,1)}, s32[4]{0:T(128)S(1)}, bf16[64,7,9,16]{3,0,2,1:T(8,128)(2,1)}, bf16[70,27,384]{2,1,0:T(8,1...) while((s32[]{:T(128)}, ...), condition=%wide.region_1.2_spmd.clone, body=%wide.region_0.1_spmd.clone.sunk | while | flops 715668608 | bytes 46324552 | solution.py:68
  38.4 1.9 %convert_bitcast_fusion.2 = bf16[7,16,11,9,27]{4,1,2,3,0:T(8,128)(2,1)S(1)} fusion(bf16[64,7,9,16]{3,0,2,1:T(8,128)(2,1)} %get-tuple-element.288, s32[]{:T(128)S(6)} %select_n.64, s32[11,27]{1,0:T(8,128)S(1)} %get-tuple-element.292), kind=kOutput, calls=%fused_computation.1.clone.1 | convolution fusion | flops 9888912 | bytes 857992 | tf_op jit(solution)/shard_map/while/body/eval_jaxpr/rqkd,lmd->qrlkm/dot_general | solution.py:50
  41.8 1.6 fusion.110
  43.5 3.1 %fusion.111 = f32[16,99,384]{2,1,0:T(8,128)} fusion(bf16[16,99,27]{2,0,1:T(8,128)(2,1)S(1)} %bitcast.61, bf16[70,27,384]{2,1,0:T(8,128)(2,1)} %get-tuple-element.289, s32[]{:T(128)S(6)} %select_n.67), kind=kOutput, calls=%fused_computation.9.clone.1 | convolution fusion | flops 32845824 | bytes 2911780 | tf_op jit(solution)/shard_map/while/body/eval_jaxpr/rxm,rmc->rxc/dot_general | solution.py:57
  46.7 3.1 %fusion.112 = f32[16,99,384]{2,1,0:T(8,128)} fusion(bf16[16,99,27]{2,0,1:T(8,128)(2,1)S(1)} %bitcast.62, bf16[70,27,384]{2,1,0:T(8,128)(2,1)} %get-tuple-element.289, s32[]{:T(128)S(6)} %select_n.68), kind=kOutput, calls=%fused_computation.11.clone.1 | convolution fusion | flops 32845824 | bytes 2911780 | tf_op jit(solution)/shard_map/while/body/eval_jaxpr/rxm,rmc->rxc/dot_general | solution.py:57
  49.8 3.1 %fusion.114 = f32[16,99,384]{2,1,0:T(8,128)} fusion(bf16[16,99,27]{2,0,1:T(8,128)(2,1)S(1)} %bitcast.64, bf16[70,27,384]{2,1,0:T(8,128)(2,1)} %get-tuple-element.289, s32[]{:T(128)S(6)} %select_n.70), kind=kOutput, calls=%fused_computation.13.clone.1 | convolution fusion | flops 32845824 | bytes 2911780 | tf_op jit(solution)/shard_map/while/body/eval_jaxpr/rxm,rmc->rxc/dot_general | solution.py:57
  53.0 3.2 %fusion.113 = f32[16,99,384]{2,1,0:T(8,128)} fusion(bf16[16,99,27]{2,0,1:T(8,128)(2,1)S(1)} %bitcast.65, bf16[70,27,384]{2,1,0:T(8,128)(2,1)} %get-tuple-element.289, s32[]{:T(128)S(6)} %select_n.69), kind=kOutput, calls=%fused_computation.15.clone.1 | convolution fusion | flops 32845824 | bytes 2911780 | tf_op jit(solution)/shard_map/while/body/eval_jaxpr/rxm,rmc->rxc/dot_general | solution.py:57
  56.2 3.1 %fusion.109 = f32[16,99,384]{2,1,0:T(8,128)} fusion(bf16[16,99,27]{2,0,1:T(8,128)(2,1)S(1)} %bitcast.63, bf16[70,27,384]{2,1,0:T(8,128)(2,1)} %get-tuple-element.289, s32[]{:T(128)S(6)} %select_n.65), kind=kOutput, calls=%fused_computation.5.clone.1 | convolution fusion | flops 32845824 | bytes 2911780 | tf_op jit(solution)/shard_map/while/body/eval_jaxpr/rxm,rmc->rxc/dot_general | solution.py:57
  59.3 6.9 %add_convert_fusion.2 = bf16[16,99,384]{2,1,0:T(8,128)(2,1)} fusion(f32[16,99,384]{2,1,0:T(8,128)} %fusion.109, f32[16,99,384]{2,1,0:T(8,128)S(1)} %fusion.110, f32[16,99,384]{2,1,0:T(8,128)} %fusion.111, f32[16,99,384]{2,1,0:T(8,128)} %fusion.112, f32[16,99,384]{2,1,0:T(8,128)} %fusion.113, f32[16,99,384]{2,1,0:T(8,128)} %fusion.114, ...), kind=kOutput, calls=%fused_computation.2.clone.1 | convolution fusion | flops 37103616 | bytes 16907812 | tf_op jit(solution)/shard_map/while/body/eval_jaxpr/rxm,rmc->rxc/dot_general | solution.py:57
  66.2 2.5 %reshape.88 = bf16[176,3456]{1,0:T(8,128)(2,1)S(1)} reshape(bf16[16,99,384]{2,1,0:T(8,128)(2,1)} %add_convert_fusion.2) | data formatting | bytes 2433024 | tf_op jit(solution)/shard_map/while/body/eval_jaxpr/reshape | solution.py:60
  68.7 3.1 %fusion.115 = bf16[176,384]{1,0:T(8,128)(2,1)S(1)} fusion(bf16[176,3456]{1,0:T(8,128)(2,1)S(1)} %reshape.88, bf16[3456,384]{1,0:T(8,128)(2,1)} %get-tuple-element.290, f32[384]{0:T(512)S(1)} %get-tuple-element.291), kind=kOutput, calls=%fused_computation.27.clone.1 | convolution fusion | flops 471601152 | bytes 4007424 | tf_op jit(solution)/shard_map/while/body/eval_jaxpr/dot_general | solution.py:61
  73.7 1.9 %convert_bitcast_fusion.2 = bf16[7,16,11,9,27]{4,1,2,3,0:T(8,128)(2,1)S(1)} fusion(bf16[64,7,9,16]{3,0,2,1:T(8,128)(2,1)} %get-tuple-element.288, s32[]{:T(128)S(6)} %select_n.64, s32[11,27]{1,0:T(8,128)S(1)} %get-tuple-element.292), kind=kOutput, calls=%fused_computation.1.clone.1 | convolution fusion | flops 9888912 | bytes 857992 | tf_op jit(solution)/shard_map/while/body/eval_jaxpr/rqkd,lmd->qrlkm/dot_general | solution.py:50
  77.1 1.6 fusion.110
  78.8 3.1 %fusion.111 = f32[16,99,384]{2,1,0:T(8,128)} fusion(bf16[16,99,27]{2,0,1:T(8,128)(2,1)S(1)} %bitcast.61, bf16[70,27,384]{2,1,0:T(8,128)(2,1)} %get-tuple-element.289, s32[]{:T(128)S(6)} %select_n.67), kind=kOutput, calls=%fused_computation.9.clone.1 | convolution fusion | flops 32845824 | bytes 2911780 | tf_op jit(solution)/shard_map/while/body/eval_jaxpr/rxm,rmc->rxc/dot_general | solution.py:57
  82.0 3.1 %fusion.112 = f32[16,99,384]{2,1,0:T(8,128)} fusion(bf16[16,99,27]{2,0,1:T(8,128)(2,1)S(1)} %bitcast.62, bf16[70,27,384]{2,1,0:T(8,128)(2,1)} %get-tuple-element.289, s32[]{:T(128)S(6)} %select_n.68), kind=kOutput, calls=%fused_computation.11.clone.1 | convolution fusion | flops 32845824 | bytes 2911780 | tf_op jit(solution)/shard_map/while/body/eval_jaxpr/rxm,rmc->rxc/dot_general | solution.py:57
  85.1 3.1 %fusion.114 = f32[16,99,384]{2,1,0:T(8,128)} fusion(bf16[16,99,27]{2,0,1:T(8,128)(2,1)S(1)} %bitcast.64, bf16[70,27,384]{2,1,0:T(8,128)(2,1)} %get-tuple-element.289, s32[]{:T(128)S(6)} %select_n.70), kind=kOutput, calls=%fused_computation.13.clone.1 | convolution fusion | flops 32845824 | bytes 2911780 | tf_op jit(solution)/shard_map/while/body/eval_jaxpr/rxm,rmc->rxc/dot_general | solution.py:57
  88.3 3.2 %fusion.113 = f32[16,99,384]{2,1,0:T(8,128)} fusion(bf16[16,99,27]{2,0,1:T(8,128)(2,1)S(1)} %bitcast.65, bf16[70,27,384]{2,1,0:T(8,128)(2,1)} %get-tuple-element.289, s32[]{:T(128)S(6)} %select_n.69), kind=kOutput, calls=%fused_computation.15.clone.1 | convolution fusion | flops 32845824 | bytes 2911780 | tf_op jit(solution)/shard_map/while/body/eval_jaxpr/rxm,rmc->rxc/dot_general | solution.py:57
  91.5 3.1 %fusion.109 = f32[16,99,384]{2,1,0:T(8,128)} fusion(bf16[16,99,27]{2,0,1:T(8,128)(2,1)S(1)} %bitcast.63, bf16[70,27,384]{2,1,0:T(8,128)(2,1)} %get-tuple-element.289, s32[]{:T(128)S(6)} %select_n.65), kind=kOutput, calls=%fused_computation.5.clone.1 | convolution fusion | flops 32845824 | bytes 2911780 | tf_op jit(solution)/shard_map/while/body/eval_jaxpr/rxm,rmc->rxc/dot_general | solution.py:57
  94.6 6.9 %add_convert_fusion.2 = bf16[16,99,384]{2,1,0:T(8,128)(2,1)} fusion(f32[16,99,384]{2,1,0:T(8,128)} %fusion.109, f32[16,99,384]{2,1,0:T(8,128)S(1)} %fusion.110, f32[16,99,384]{2,1,0:T(8,128)} %fusion.111, f32[16,99,384]{2,1,0:T(8,128)} %fusion.112, f32[16,99,384]{2,1,0:T(8,128)} %fusion.113, f32[16,99,384]{2,1,0:T(8,128)} %fusion.114, ...), kind=kOutput, calls=%fused_computation.2.clone.1 | convolution fusion | flops 37103616 | bytes 16907812 | tf_op jit(solution)/shard_map/while/body/eval_jaxpr/rxm,rmc->rxc/dot_general | solution.py:57
  101.5 2.5 %reshape.88 = bf16[176,3456]{1,0:T(8,128)(2,1)S(1)} reshape(bf16[16,99,384]{2,1,0:T(8,128)(2,1)} %add_convert_fusion.2) | data formatting | bytes 2433024 | tf_op jit(solution)/shard_map/while/body/eval_jaxpr/reshape | solution.py:60
  104.0 3.1 %fusion.115 = bf16[176,384]{1,0:T(8,128)(2,1)S(1)} fusion(bf16[176,3456]{1,0:T(8,128)(2,1)S(1)} %reshape.88, bf16[3456,384]{1,0:T(8,128)(2,1)} %get-tuple-element.290, f32[384]{0:T(512)S(1)} %get-tuple-element.291), kind=kOutput, calls=%fused_computation.27.clone.1 | convolution fusion | flops 471601152 | bytes 4007424 | tf_op jit(solution)/shard_map/while/body/eval_jaxpr/dot_general | solution.py:61
  109.0 1.9 %convert_bitcast_fusion.2 = bf16[7,16,11,9,27]{4,1,2,3,0:T(8,128)(2,1)S(1)} fusion(bf16[64,7,9,16]{3,0,2,1:T(8,128)(2,1)} %get-tuple-element.288, s32[]{:T(128)S(6)} %select_n.64, s32[11,27]{1,0:T(8,128)S(1)} %get-tuple-element.292), kind=kOutput, calls=%fused_computation.1.clone.1 | convolution fusion | flops 9888912 | bytes 857992 | tf_op jit(solution)/shard_map/while/body/eval_jaxpr/rqkd,lmd->qrlkm/dot_general | solution.py:50
  112.4 1.6 fusion.110
  114.1 3.1 %fusion.111 = f32[16,99,384]{2,1,0:T(8,128)} fusion(bf16[16,99,27]{2,0,1:T(8,128)(2,1)S(1)} %bitcast.61, bf16[70,27,384]{2,1,0:T(8,128)(2,1)} %get-tuple-element.289, s32[]{:T(128)S(6)} %select_n.67), kind=kOutput, calls=%fused_computation.9.clone.1 | convolution fusion | flops 32845824 | bytes 2911780 | tf_op jit(solution)/shard_map/while/body/eval_jaxpr/rxm,rmc->rxc/dot_general | solution.py:57
  117.3 3.1 %fusion.112 = f32[16,99,384]{2,1,0:T(8,128)} fusion(bf16[16,99,27]{2,0,1:T(8,128)(2,1)S(1)} %bitcast.62, bf16[70,27,384]{2,1,0:T(8,128)(2,1)} %get-tuple-element.289, s32[]{:T(128)S(6)} %select_n.68), kind=kOutput, calls=%fused_computation.11.clone.1 | convolution fusion | flops 32845824 | bytes 2911780 | tf_op jit(solution)/shard_map/while/body/eval_jaxpr/rxm,rmc->rxc/dot_general | solution.py:57
  120.5 3.1 %fusion.114 = f32[16,99,384]{2,1,0:T(8,128)} fusion(bf16[16,99,27]{2,0,1:T(8,128)(2,1)S(1)} %bitcast.64, bf16[70,27,384]{2,1,0:T(8,128)(2,1)} %get-tuple-element.289, s32[]{:T(128)S(6)} %select_n.70), kind=kOutput, calls=%fused_computation.13.clone.1 | convolution fusion | flops 32845824 | bytes 2911780 | tf_op jit(solution)/shard_map/while/body/eval_jaxpr/rxm,rmc->rxc/dot_general | solution.py:57
  123.6 3.2 %fusion.113 = f32[16,99,384]{2,1,0:T(8,128)} fusion(bf16[16,99,27]{2,0,1:T(8,128)(2,1)S(1)} %bitcast.65, bf16[70,27,384]{2,1,0:T(8,128)(2,1)} %get-tuple-element.289, s32[]{:T(128)S(6)} %select_n.69), kind=kOutput, calls=%fused_computation.15.clone.1 | convolution fusion | flops 32845824 | bytes 2911780 | tf_op jit(solution)/shard_map/while/body/eval_jaxpr/rxm,rmc->rxc/dot_general | solution.py:57
  126.8 3.1 %fusion.109 = f32[16,99,384]{2,1,0:T(8,128)} fusion(bf16[16,99,27]{2,0,1:T(8,128)(2,1)S(1)} %bitcast.63, bf16[70,27,384]{2,1,0:T(8,128)(2,1)} %get-tuple-element.289, s32[]{:T(128)S(6)} %select_n.65), kind=kOutput, calls=%fused_computation.5.clone.1 | convolution fusion | flops 32845824 | bytes 2911780 | tf_op jit(solution)/shard_map/while/body/eval_jaxpr/rxm,rmc->rxc/dot_general | solution.py:57
  130.0 6.9 %add_convert_fusion.2 = bf16[16,99,384]{2,1,0:T(8,128)(2,1)} fusion(f32[16,99,384]{2,1,0:T(8,128)} %fusion.109, f32[16,99,384]{2,1,0:T(8,128)S(1)} %fusion.110, f32[16,99,384]{2,1,0:T(8,128)} %fusion.111, f32[16,99,384]{2,1,0:T(8,128)} %fusion.112, f32[16,99,384]{2,1,0:T(8,128)} %fusion.113, f32[16,99,384]{2,1,0:T(8,128)} %fusion.114, ...), kind=kOutput, calls=%fused_computation.2.clone.1 | convolution fusion | flops 37103616 | bytes 16907812 | tf_op jit(solution)/shard_map/while/body/eval_jaxpr/rxm,rmc->rxc/dot_general | solution.py:57
  136.8 2.5 %reshape.88 = bf16[176,3456]{1,0:T(8,128)(2,1)S(1)} reshape(bf16[16,99,384]{2,1,0:T(8,128)(2,1)} %add_convert_fusion.2) | data formatting | bytes 2433024 | tf_op jit(solution)/shard_map/while/body/eval_jaxpr/reshape | solution.py:60
  139.4 3.1 %fusion.115 = bf16[176,384]{1,0:T(8,128)(2,1)S(1)} fusion(bf16[176,3456]{1,0:T(8,128)(2,1)S(1)} %reshape.88, bf16[3456,384]{1,0:T(8,128)(2,1)} %get-tuple-element.290, f32[384]{0:T(512)S(1)} %get-tuple-element.291), kind=kOutput, calls=%fused_computation.27.clone.1 | convolution fusion | flops 471601152 | bytes 4007424 | tf_op jit(solution)/shard_map/while/body/eval_jaxpr/dot_general | solution.py:61
  144.4 1.9 %convert_bitcast_fusion.2 = bf16[7,16,11,9,27]{4,1,2,3,0:T(8,128)(2,1)S(1)} fusion(bf16[64,7,9,16]{3,0,2,1:T(8,128)(2,1)} %get-tuple-element.288, s32[]{:T(128)S(6)} %select_n.64, s32[11,27]{1,0:T(8,128)S(1)} %get-tuple-element.292), kind=kOutput, calls=%fused_computation.1.clone.1 | convolution fusion | flops 9888912 | bytes 857992 | tf_op jit(solution)/shard_map/while/body/eval_jaxpr/rqkd,lmd->qrlkm/dot_general | solution.py:50
  147.8 1.6 fusion.110
  149.5 3.1 %fusion.111 = f32[16,99,384]{2,1,0:T(8,128)} fusion(bf16[16,99,27]{2,0,1:T(8,128)(2,1)S(1)} %bitcast.61, bf16[70,27,384]{2,1,0:T(8,128)(2,1)} %get-tuple-element.289, s32[]{:T(128)S(6)} %select_n.67), kind=kOutput, calls=%fused_computation.9.clone.1 | convolution fusion | flops 32845824 | bytes 2911780 | tf_op jit(solution)/shard_map/while/body/eval_jaxpr/rxm,rmc->rxc/dot_general | solution.py:57
  152.6 3.1 %fusion.112 = f32[16,99,384]{2,1,0:T(8,128)} fusion(bf16[16,99,27]{2,0,1:T(8,128)(2,1)S(1)} %bitcast.62, bf16[70,27,384]{2,1,0:T(8,128)(2,1)} %get-tuple-element.289, s32[]{:T(128)S(6)} %select_n.68), kind=kOutput, calls=%fused_computation.11.clone.1 | convolution fusion | flops 32845824 | bytes 2911780 | tf_op jit(solution)/shard_map/while/body/eval_jaxpr/rxm,rmc->rxc/dot_general | solution.py:57
  155.8 3.1 %fusion.114 = f32[16,99,384]{2,1,0:T(8,128)} fusion(bf16[16,99,27]{2,0,1:T(8,128)(2,1)S(1)} %bitcast.64, bf16[70,27,384]{2,1,0:T(8,128)(2,1)} %get-tuple-element.289, s32[]{:T(128)S(6)} %select_n.70), kind=kOutput, calls=%fused_computation.13.clone.1 | convolution fusion | flops 32845824 | bytes 2911780 | tf_op jit(solution)/shard_map/while/body/eval_jaxpr/rxm,rmc->rxc/dot_general | solution.py:57
  159.0 3.2 %fusion.113 = f32[16,99,384]{2,1,0:T(8,128)} fusion(bf16[16,99,27]{2,0,1:T(8,128)(2,1)S(1)} %bitcast.65, bf16[70,27,384]{2,1,0:T(8,128)(2,1)} %get-tuple-element.289, s32[]{:T(128)S(6)} %select_n.69), kind=kOutput, calls=%fused_computation.15.clone.1 | convolution fusion | flops 32845824 | bytes 2911780 | tf_op jit(solution)/shard_map/while/body/eval_jaxpr/rxm,rmc->rxc/dot_general | solution.py:57
  162.2 3.1 %fusion.109 = f32[16,99,384]{2,1,0:T(8,128)} fusion(bf16[16,99,27]{2,0,1:T(8,128)(2,1)S(1)} %bitcast.63, bf16[70,27,384]{2,1,0:T(8,128)(2,1)} %get-tuple-element.289, s32[]{:T(128)S(6)} %select_n.65), kind=kOutput, calls=%fused_computation.5.clone.1 | convolution fusion | flops 32845824 | bytes 2911780 | tf_op jit(solution)/shard_map/while/body/eval_jaxpr/rxm,rmc->rxc/dot_general | solution.py:57
  165.3 6.9 %add_convert_fusion.2 = bf16[16,99,384]{2,1,0:T(8,128)(2,1)} fusion(f32[16,99,384]{2,1,0:T(8,128)} %fusion.109, f32[16,99,384]{2,1,0:T(8,128)S(1)} %fusion.110, f32[16,99,384]{2,1,0:T(8,128)} %fusion.111, f32[16,99,384]{2,1,0:T(8,128)} %fusion.112, f32[16,99,384]{2,1,0:T(8,128)} %fusion.113, f32[16,99,384]{2,1,0:T(8,128)} %fusion.114, ...), kind=kOutput, calls=%fused_computation.2.clone.1 | convolution fusion | flops 37103616 | bytes 16907812 | tf_op jit(solution)/shard_map/while/body/eval_jaxpr/rxm,rmc->rxc/dot_general | solution.py:57
  172.2 2.5 %reshape.88 = bf16[176,3456]{1,0:T(8,128)(2,1)S(1)} reshape(bf16[16,99,384]{2,1,0:T(8,128)(2,1)} %add_convert_fusion.2) | data formatting | bytes 2433024 | tf_op jit(solution)/shard_map/while/body/eval_jaxpr/reshape | solution.py:60
  174.7 3.1 %fusion.115 = bf16[176,384]{1,0:T(8,128)(2,1)S(1)} fusion(bf16[176,3456]{1,0:T(8,128)(2,1)S(1)} %reshape.88, bf16[3456,384]{1,0:T(8,128)(2,1)} %get-tuple-element.290, f32[384]{0:T(512)S(1)} %get-tuple-element.291), kind=kOutput, calls=%fused_computation.27.clone.1 | convolution fusion | flops 471601152 | bytes 4007424 | tf_op jit(solution)/shard_map/while/body/eval_jaxpr/dot_general | solution.py:61
  (107 shorter events, 21.8 us)
Async XLA Ops:
  1.0 9.2 %collective-permute-start = (bf16[3,11,384]{2,1,0:T(8,128)(2,1)S(1)}, bf16[3,11,384]{2,1,0:T(8,128)(2,1)S(1)}, u32[]{:S(2)}, u32[]{:S(2)}) collective-permute-start(bf16[3,11,384]{2,1,0:T(8,128)(2,1)S(1)} %copy.61), channel_id=1, source_target_pairs={{0,1},{2,3},{4,5},{6,7},{8,9},{10,11},{12,13},{14,15},{16,17},{18,... | collective-permute-start | bytes 76040 | tf_op jit(solution)/shard_map/ppermute | solution.py:20
  2.3 9.4 %collective-permute-start.1 = (bf16[3,11,384]{2,1,0:T(8,128)(2,1)S(1)}, bf16[3,11,384]{2,1,0:T(8,128)(2,1)S(1)}, u32[]{:S(2)}, u32[]{:S(2)}) collective-permute-start(bf16[3,11,384]{2,1,0:T(8,128)(2,1)S(1)} %copy.62), channel_id=1, source_target_pairs={{1,0},{3,2},{5,4},{7,6},{9,8},{11,10},{13,12},{15,14},{17,16},{19,... | collective-permute-start | bytes 76040 | tf_op jit(solution)/shard_map/ppermute | solution.py:21
  12.6 21.1 %collective-permute-start.2 = (bf16[70,8,384]{2,1,0:T(8,128)(2,1)}, bf16[70,8,384]{2,1,0:T(8,128)(2,1)S(1)}, u32[]{:S(2)}, u32[]{:S(2)}) collective-permute-start(bf16[70,8,384]{2,1,0:T(8,128)(2,1)} %get-tuple-element.170), channel_id=1, source_target_pairs={{0,2},{2,4},{4,6},{6,8},{8,10},{10,12},{12,14},{14,0},{1,3},{3,5},... | collective-permute-start | bytes 1290248 | tf_op jit(solution)/shard_map/ppermute | solution.py:20
  14.7 21.0 %collective-permute-start.3 = (bf16[70,8,384]{2,1,0:T(8,128)(2,1)S(1)}, bf16[70,8,384]{2,1,0:T(8,128)(2,1)S(1)}, u32[]{:S(2)}, u32[]{:S(2)}) collective-permute-start(bf16[70,8,384]{2,1,0:T(8,128)(2,1)S(1)} %get-tuple-element.171), channel_id=1, source_target_pairs={{2,0},{4,2},{6,4},{8,6},{10,8},{12,10},{14,12},{0,14},{3,1},{5,3},... | collective-permute-start | bytes 1290248 | tf_op jit(solution)/shard_map/ppermute | solution.py:21
  20.4 16.9 %copy-start.5 = (f32[384]{0:T(512)S(1)}, f32[384]{0:T(512)}, u32[]{:S(2)}) copy-start(f32[384]{0:T(512)} %param.17) | copy-start | bytes 4612
  41.8 1.6 copy-start.4
  43.5 3.1 %copy-start.3 = (bf16[1,16,11,9,27]{4,1,2,3,0:T(8,128)(2,1)S(1)}, bf16[1,16,11,9,27]{4,1,2,3,0:T(8,128)(2,1)}, u32[]{:S(2)}) copy-start(bf16[1,16,11,9,27]{4,1,2,3,0:T(8,128)(2,1)} %get-tuple-element.233) | copy-start | bytes 256612 | tf_op jit(solution)/shard_map/while
  46.6 3.1 %copy-start.2 = (bf16[1,16,11,9,27]{4,1,2,3,0:T(8,128)(2,1)S(1)}, bf16[1,16,11,9,27]{4,1,2,3,0:T(8,128)(2,1)}, u32[]{:S(2)}) copy-start(bf16[1,16,11,9,27]{4,1,2,3,0:T(8,128)(2,1)} %get-tuple-element.235) | copy-start | bytes 256612 | tf_op jit(solution)/shard_map/while
  49.8 3.1 %copy-start.1 = (bf16[1,16,11,9,27]{4,1,2,3,0:T(8,128)(2,1)S(1)}, bf16[1,16,11,9,27]{4,1,2,3,0:T(8,128)(2,1)}, u32[]{:S(2)}) copy-start(bf16[1,16,11,9,27]{4,1,2,3,0:T(8,128)(2,1)} %get-tuple-element.234) | copy-start | bytes 256612 | tf_op jit(solution)/shard_map/while
  53.0 3.2 %copy-start = (bf16[1,16,11,9,27]{4,1,2,3,0:T(8,128)(2,1)S(1)}, bf16[1,16,11,9,27]{4,1,2,3,0:T(8,128)(2,1)}, u32[]{:S(2)}) copy-start(bf16[1,16,11,9,27]{4,1,2,3,0:T(8,128)(2,1)} %get-tuple-element.230) | copy-start | bytes 256612 | tf_op jit(solution)/shard_map/while
  77.1 1.6 copy-start.4
  78.8 3.1 %copy-start.3 = (bf16[1,16,11,9,27]{4,1,2,3,0:T(8,128)(2,1)S(1)}, bf16[1,16,11,9,27]{4,1,2,3,0:T(8,128)(2,1)}, u32[]{:S(2)}) copy-start(bf16[1,16,11,9,27]{4,1,2,3,0:T(8,128)(2,1)} %get-tuple-element.233) | copy-start | bytes 256612 | tf_op jit(solution)/shard_map/while
  82.0 3.1 %copy-start.2 = (bf16[1,16,11,9,27]{4,1,2,3,0:T(8,128)(2,1)S(1)}, bf16[1,16,11,9,27]{4,1,2,3,0:T(8,128)(2,1)}, u32[]{:S(2)}) copy-start(bf16[1,16,11,9,27]{4,1,2,3,0:T(8,128)(2,1)} %get-tuple-element.235) | copy-start | bytes 256612 | tf_op jit(solution)/shard_map/while
  85.1 3.1 %copy-start.1 = (bf16[1,16,11,9,27]{4,1,2,3,0:T(8,128)(2,1)S(1)}, bf16[1,16,11,9,27]{4,1,2,3,0:T(8,128)(2,1)}, u32[]{:S(2)}) copy-start(bf16[1,16,11,9,27]{4,1,2,3,0:T(8,128)(2,1)} %get-tuple-element.234) | copy-start | bytes 256612 | tf_op jit(solution)/shard_map/while
  88.3 3.2 %copy-start = (bf16[1,16,11,9,27]{4,1,2,3,0:T(8,128)(2,1)S(1)}, bf16[1,16,11,9,27]{4,1,2,3,0:T(8,128)(2,1)}, u32[]{:S(2)}) copy-start(bf16[1,16,11,9,27]{4,1,2,3,0:T(8,128)(2,1)} %get-tuple-element.230) | copy-start | bytes 256612 | tf_op jit(solution)/shard_map/while
  112.4 1.6 copy-start.4
  114.1 3.1 %copy-start.3 = (bf16[1,16,11,9,27]{4,1,2,3,0:T(8,128)(2,1)S(1)}, bf16[1,16,11,9,27]{4,1,2,3,0:T(8,128)(2,1)}, u32[]{:S(2)}) copy-start(bf16[1,16,11,9,27]{4,1,2,3,0:T(8,128)(2,1)} %get-tuple-element.233) | copy-start | bytes 256612 | tf_op jit(solution)/shard_map/while
  117.3 3.1 %copy-start.2 = (bf16[1,16,11,9,27]{4,1,2,3,0:T(8,128)(2,1)S(1)}, bf16[1,16,11,9,27]{4,1,2,3,0:T(8,128)(2,1)}, u32[]{:S(2)}) copy-start(bf16[1,16,11,9,27]{4,1,2,3,0:T(8,128)(2,1)} %get-tuple-element.235) | copy-start | bytes 256612 | tf_op jit(solution)/shard_map/while
  120.5 3.1 %copy-start.1 = (bf16[1,16,11,9,27]{4,1,2,3,0:T(8,128)(2,1)S(1)}, bf16[1,16,11,9,27]{4,1,2,3,0:T(8,128)(2,1)}, u32[]{:S(2)}) copy-start(bf16[1,16,11,9,27]{4,1,2,3,0:T(8,128)(2,1)} %get-tuple-element.234) | copy-start | bytes 256612 | tf_op jit(solution)/shard_map/while
  123.6 3.2 %copy-start = (bf16[1,16,11,9,27]{4,1,2,3,0:T(8,128)(2,1)S(1)}, bf16[1,16,11,9,27]{4,1,2,3,0:T(8,128)(2,1)}, u32[]{:S(2)}) copy-start(bf16[1,16,11,9,27]{4,1,2,3,0:T(8,128)(2,1)} %get-tuple-element.230) | copy-start | bytes 256612 | tf_op jit(solution)/shard_map/while
  147.8 1.6 copy-start.4
  149.5 3.1 %copy-start.3 = (bf16[1,16,11,9,27]{4,1,2,3,0:T(8,128)(2,1)S(1)}, bf16[1,16,11,9,27]{4,1,2,3,0:T(8,128)(2,1)}, u32[]{:S(2)}) copy-start(bf16[1,16,11,9,27]{4,1,2,3,0:T(8,128)(2,1)} %get-tuple-element.233) | copy-start | bytes 256612 | tf_op jit(solution)/shard_map/while
  152.6 3.1 %copy-start.2 = (bf16[1,16,11,9,27]{4,1,2,3,0:T(8,128)(2,1)S(1)}, bf16[1,16,11,9,27]{4,1,2,3,0:T(8,128)(2,1)}, u32[]{:S(2)}) copy-start(bf16[1,16,11,9,27]{4,1,2,3,0:T(8,128)(2,1)} %get-tuple-element.235) | copy-start | bytes 256612 | tf_op jit(solution)/shard_map/while
  155.8 3.1 %copy-start.1 = (bf16[1,16,11,9,27]{4,1,2,3,0:T(8,128)(2,1)S(1)}, bf16[1,16,11,9,27]{4,1,2,3,0:T(8,128)(2,1)}, u32[]{:S(2)}) copy-start(bf16[1,16,11,9,27]{4,1,2,3,0:T(8,128)(2,1)} %get-tuple-element.234) | copy-start | bytes 256612 | tf_op jit(solution)/shard_map/while
  159.0 3.2 %copy-start = (bf16[1,16,11,9,27]{4,1,2,3,0:T(8,128)(2,1)S(1)}, bf16[1,16,11,9,27]{4,1,2,3,0:T(8,128)(2,1)}, u32[]{:S(2)}) copy-start(bf16[1,16,11,9,27]{4,1,2,3,0:T(8,128)(2,1)} %get-tuple-element.230) | copy-start | bytes 256612 | tf_op jit(solution)/shard_map/while
where the time goes:
time: 180 us; the launch traced here: 179 us
  matrix products  119 us (66%)
  local copies, waits for them, and re-layouts  30 us (17%)
  waiting for transfers between devices  14 us (8%)
  starting transfers between devices  9.4 us (5%)
  other arithmetic  3.08 us (2%)
  loops' own time  2.98 us (2%)
    dot_general x28, matrix products, one_block(): jnp.einsum('rxm,rmc->rxc', band[offset_row], source, preferred_element_ty...  96.3 us
    dot_general x4, matrix products, one_block(): pre_act = jnp.dot(conv, mixing, preferred_element_type=jnp.float32) + bias  12.4 us
    ppermute x2, waiting for transfers between devices, padded(): before = lax.ppermute(last, axis, up)  12.1 us
    reshape x4, local copies, waits for them, and re-layouts, one_block(): conv_sum.astype(jnp.bfloat16).reshape(block_rows * cols, BASIS * width)  10.1 us
    dot_general x4, matrix products, one_block(): jnp.einsum('rqkd,lmd->qrlkm', block_profile, band_hot, preferred_element_...  7.6 us
    slice x32, local copies, waits for them, and re-layouts, one_block(): band[offset_row]  6.54 us
    ppermute x2, starting transfers between devices, padded(): after = lax.ppermute(leading, axis, down)  6.07 us
  transfers between devices with their start and end apart: 4, of which 2 were waited for; matrix products, arithmetic and copies ran while one was open for 6% of the time, Pallas kernels for 0%

commit v1 on v0

v1 whole, which is shorter than its diff:
```python
import functools

import jax
import jax.numpy as jnp
from jax import lax
from jax.experimental import pallas as pl
from jax.experimental.pallas import tpu as pltpu
from jax.sharding import PartitionSpec as P

BASIS = 9
RAD = 3
BLOCK = 4
SLOTS = 16
HALO = 8
ROWS = 16
MESH = pl.DeviceIdType.MESH


def kernel(
    lon_size,
    x_ref,
    rows_ref,
    cols_ref,
    reach_ref,
    counts_ref,
    filt_ref,
    mix_ref,
    bias_ref,
    out_ref,
    ext,
    mix,
    hot,
    taps,
    near,
    far,
    conv,
    own_sem,
    mix_sem,
    pair_send,
    pair_recv,
    fwd_send,
    fwd_recv,
    lat_send,
    lat_recv,
):
    cols, rows, width = x_ref.shape
    chunks = rows // ROWS
    lon = lax.axis_index("lon")
    lat = lax.axis_index("lat")
    even = lax.rem(lon, 2) == 0
    partner = jnp.where(even, lon + 1, lon - 1)
    ahead = lax.rem(lon + 2, lon_size)
    behind = lax.rem(lon + lon_size - 2, lon_size)
    onward = jnp.where(even, ahead, behind)
    other = 1 - lat

    def chunk_at(step):
        return jnp.where(lat == 0, chunks - 1 - step, step)

    def rows_at(start):
        return pl.ds(pl.multiple_of(start, ROWS), ROWS)

    own_copy = pltpu.make_async_copy(
        x_ref, ext.at[pl.ds(cols, cols), pl.ds(ROWS, rows), :], own_sem
    )
    own_copy.start()
    mix_copy = pltpu.make_async_copy(mix_ref, mix, mix_sem)
    mix_copy.start()

    barrier = pltpu.get_barrier_semaphore()
    for target in ({"lon": partner}, {"lon": ahead}, {"lon": behind}, {"lat": other}):
        pl.semaphore_signal(barrier, inc=1, device_id=target, device_id_type=MESH)
    pl.semaphore_wait(barrier, 4)

    there = jnp.where(even, 0, 2 * cols)
    here = 2 * cols - there
    fwd_from = jnp.where(even, here + cols - HALO, here)
    fwd_to = jnp.where(even, cols - HALO, 2 * cols)

    def pair_copy(step):
        first = chunk_at(step) * ROWS
        return pltpu.make_async_remote_copy(
            src_ref=x_ref.at[:, rows_at(first), :],
            dst_ref=ext.at[pl.ds(there, cols), rows_at(first + ROWS), :],
            send_sem=pair_send.at[step],
            recv_sem=pair_recv.at[step],
            device_id={"lon": partner},
            device_id_type=MESH,
        )

    def fwd_copy(step):
        first = chunk_at(step) * ROWS + ROWS
        return pltpu.make_async_remote_copy(
            src_ref=ext.at[pl.ds(fwd_from, HALO), rows_at(first), :],
            dst_ref=ext.at[pl.ds(fwd_to, HALO), rows_at(first), :],
            send_sem=fwd_send.at[step],
            recv_sem=fwd_recv.at[step],
            device_id={"lon": onward},
            device_id_type=MESH,
        )

    edge = chunk_at(0) * ROWS
    edge_there = jnp.where(lat == 0, 0, rows + ROWS)

    def lat_copy(which, source, first, count, start):
        return pltpu.make_async_remote_copy(
            src_ref=source,
            dst_ref=ext.at[pl.ds(first, count), rows_at(edge_there), :],
            send_sem=lat_send.at[which],
            recv_sem=lat_recv.at[which],
            device_id={"lat": other},
            device_id_type=MESH,
        )

    lat_own = lat_copy(0, x_ref.at[:, rows_at(edge), :], cols, cols, edge)
    lat_pair = lat_copy(
        1, ext.at[pl.ds(here, cols), rows_at(edge + ROWS), :], here, cols, edge
    )
    lat_fwd = lat_copy(
        2, ext.at[pl.ds(fwd_to, HALO), rows_at(edge + ROWS), :], fwd_to, HALO, edge
    )

    pairs = [pair_copy(step) for step in range(chunks)]
    fwds = [fwd_copy(step) for step in range(chunks)]
    for copy in pairs:
        copy.start()
    lat_own.start()

    beyond = jnp.where(lat == 0, 0, rows + ROWS)
    ext[:, rows_at(beyond), :] = jnp.zeros((3 * cols, ROWS, width), ext.dtype)

    at = lax.broadcasted_iota(jnp.int32, (128, 256), 0)
    lane = lax.broadcasted_iota(jnp.int32, (128, 256), 1)
    same_col = (lane >> 4) == ((at >> 3) & 3) * BLOCK + (at >> 5)
    for row in range(8):
        same = same_col & ((lane & 15) == (((at & 7) + row - RAD) & 15))
        hot[row] = jnp.where(same, 1.0, 0.0).astype(jnp.bfloat16)

    slot = lax.broadcasted_iota(jnp.int32, (SLOTS, rows), 0)
    code = (cols_ref[...] - reach_ref[...] + 2) * 8 + rows_ref[...]
    code = jnp.where(slot < counts_ref[...], code, -1)
    place = lax.broadcasted_iota(jnp.int32, (32, rows), 0)
    row_of = lax.broadcasted_iota(jnp.int32, (rows, 256), 0)
    lane_of = lax.broadcasted_iota(jnp.int32, (rows, 256), 1)

    def build(k, carry):
        parts = []
        for t in range(BLOCK):
            values = filt_ref[k * BLOCK + t].astype(jnp.float32)
            total = jnp.zeros((32, rows), jnp.float32)
            for s in range(SLOTS):
                total += jnp.where(place == code[s : s + 1, :], values[s : s + 1, :], 0.0)
            parts.append(total)
        profile = jnp.concatenate(parts, axis=0).astype(jnp.bfloat16)
        result = jnp.zeros((rows, 256), jnp.float32)
        for row in range(8):
            spread = lax.dot_general(
                profile,
                hot[row],
                (((0,), (0,)), ((), ())),
                preferred_element_type=jnp.float32,
            )
            result = jnp.where((row_of & 7) == row, spread, result)
        turned = jnp.where(
            (lane_of & 15) < 8, pltpu.roll(result, 248, 1), pltpu.roll(result, 8, 1)
        )
        taps[k] = jnp.where((row_of & 8) == 8, turned, result)
        return carry

    lax.fori_loop(0, BASIS, build, 0)
    own_copy.wait()
    mix_copy.wait()

    low = cols - HALO
    span = cols + 2 * HALO - 1
    row16 = lax.broadcasted_iota(jnp.int32, (span, ROWS, width), 1)

    def compute(step):
        first = pl.multiple_of(chunk_at(step) * ROWS, ROWS)
        held = pl.ds(low, span)
        before = ext[held, pl.ds(first, ROWS), :].astype(jnp.float32)
        middle = ext[held, pl.ds(pl.multiple_of(first + ROWS, ROWS), ROWS), :].astype(jnp.float32)
        after = ext[held, pl.ds(pl.multiple_of(first + 2 * ROWS, ROWS), ROWS), :].astype(jnp.float32)
        near[...] = jnp.where(row16 < 12, middle, before).astype(jnp.bfloat16)
        far[...] = jnp.where(row16 < 4, after, middle).astype(jnp.bfloat16)
        tap = taps[:, pl.ds(first, ROWS), :]
        tap_near = tap[:, :8, :].reshape(BASIS * 8, 256).astype(jnp.bfloat16)
        tap_far = tap[:, 8:, :].reshape(BASIS * 8, 256).astype(jnp.bfloat16)
        for col in range(cols):
            sums = [
                jnp.dot(
                    tap_part,
                    source[col : col + 16].reshape(256, width),
                    preferred_element_type=jnp.float32,
                )
                for tap_part, source in ((tap_near, near), (tap_far, far))
            ]
            for k in range(BASIS):
                both = jnp.concatenate([part[8 * k : 8 * k + 8] for part in sums], axis=0)
                conv[col * ROWS : (col + 1) * ROWS, k * width : (k + 1) * width] = both.astype(
                    jnp.bfloat16
                )
        pre = jnp.dot(conv[...], mix[...], preferred_element_type=jnp.float32) + bias_ref[...]
        act = pre * (1.0 + lax.erf(pre * (0.5**0.5))) * 0.5
        out_ref[:, pl.ds(first, ROWS), :] = act.astype(jnp.bfloat16).reshape(cols, ROWS, width)

    for step in range(chunks):
        pairs[step].wait_recv()
        fwds[step].start()
        if step == 0:
            lat_pair.start()
            lat_own.wait_recv()
            fwds[0].wait_recv()
            lat_fwd.start()
            lat_pair.wait_recv()
            lat_fwd.wait_recv()
        else:
            fwds[step].wait_recv()
            compute(step - 1)
    compute(chunks - 1)
    for copy in pairs + fwds + [lat_own, lat_pair, lat_fwd]:
        copy.wait_send()


def body(lon_size, field, reach, slot_rows, slot_cols, counts, filters, mixing, bias):
    rows, cols, width = field.shape
    chunks = rows // ROWS
    vmem = pl.BlockSpec(memory_space=pltpu.VMEM)
    anywhere = pl.BlockSpec(memory_space=pl.ANY)
    dma = pltpu.SemaphoreType.DMA
    span = cols + 2 * HALO - 1
    out = pl.pallas_call(
        functools.partial(kernel, lon_size),
        out_shape=jax.ShapeDtypeStruct((cols, rows, width), jnp.bfloat16),
        in_specs=[anywhere, vmem, vmem, vmem, vmem, vmem, anywhere, vmem],
        out_specs=vmem,
        scratch_shapes=[
            pltpu.VMEM((3 * cols, rows + 2 * ROWS, width), jnp.bfloat16),
            pltpu.VMEM(mixing.shape, jnp.bfloat16),
            pltpu.VMEM((8, 128, 256), jnp.bfloat16),
            pltpu.VMEM((BASIS, rows, 256), jnp.float32),
            pltpu.VMEM((span, ROWS, width), jnp.bfloat16),
            pltpu.VMEM((span, ROWS, width), jnp.bfloat16),
            pltpu.VMEM((cols * ROWS, BASIS * width), jnp.bfloat16),
            dma,
            dma,
            dma((chunks,)),
            dma((chunks,)),
            dma((chunks,)),
            dma((chunks,)),
            dma((3,)),
            dma((3,)),
        ],
        compiler_params=pltpu.CompilerParams(
            collective_id=0, has_side_effects=True, vmem_limit_bytes=48 * 2**20
        ),
    )(
        field.transpose(1, 0, 2),
        slot_rows.T,
        slot_cols.T,
        reach[None, :],
        counts[None, :],
        filters.transpose(2, 1, 0),
        mixing,
        bias[None, :],
    )
    return out.transpose(1, 0, 2)


def solution(mesh):
    return jax.shard_map(
        functools.partial(body, mesh.shape["lon"]),
        mesh=mesh,
        in_specs=(
            P(("members", "lat"), "lon", None),
            P("lat"),
            P("lat", None),
            P("lat", None),
            P("lat"),
            P("lat", None, None),
            P(),
            P(),
        ),
        out_specs=P(("members", "lat"), "lon", None),
        check_vma=False,
    )
```

time: 180 us -> 42.9 us (0.24)
  the two profiles are of different devices: /device:TPU:1 before, /device:TPU:0 now
where the time goes in v1:
time: 42.9 us; the launch traced here: 42.6 us
  Pallas kernels  34.7 us (81%)
  local copies, waits for them, and re-layouts  7.89 us (18%)
    pallas_call x1, Pallas kernels, body(): pl.pallas_call(functools.partial(kernel, lon_size), out_shape=jax.ShapeDt...  34.7 us
    unnamed x15, local copies, waits for them, and re-layouts  7.21 us

profile of v1, /device:TPU:0, one launch (start us, length us, event | category | flops | bytes accessed | tf_op | source)
XLA Modules:
  0.0 42.6 jit_solution(16111273836397890990)
XLA Ops:
  0.0 0.7 %broadcast_in_dim.11.bias_ref = f32[1,384]{1,0:T(1,128)S(1)} reshape(f32[384]{0:T(512)} %param.15) | data formatting | bytes 3072 | tf_op jit(solution)/shard_map/broadcast_in_dim | solution.py:265
  0.7 0.0 copy-start
  0.7 1.7 %copy-done = bf16[3456,384]{1,0:T(8,128)(2,1)S(1)} copy-done((bf16[3456,384]{1,0:T(8,128)(2,1)S(1)}, bf16[3456,384]{1,0:T(8,128)(2,1)}, u32[]{:S(2)}) %copy-start) | copy-done | bytes 2654232
  2.4 0.0 copy-start.1
  2.4 1.0 %copy-done.1 = bf16[64,11,384]{2,0,1:T(8,128)(2,1)S(1)} copy-done((bf16[64,11,384]{2,0,1:T(8,128)(2,1)S(1)}, bf16[64,11,384]{2,0,1:T(8,128)(2,1)}, u32[]{:S(2)}) %copy-start.1) | copy-done | bytes 540696
  3.5 0.0 copy-start.2
  3.5 0.9 %copy-done.2 = bf16[64,16,36]{0,1,2:T(8,128)(2,1)S(1)} copy-done((bf16[64,16,36]{0,1,2:T(8,128)(2,1)S(1)}, bf16[64,16,36]{0,1,2:T(8,128)(2,1)}, u32[]{:S(2)}) %copy-start.2) | copy-done | bytes 73752
  4.4 0.0 copy-start.3
  4.4 0.7 %copy-done.3 = s32[64,16]{0,1:T(8,128)S(1)} copy-done((s32[64,16]{0,1:T(8,128)S(1)}, s32[64,16]{0,1:T(8,128)}, u32[]{:S(2)}) %copy-start.3) | copy-done | bytes 4120
  5.1 0.0 copy-start.4
  5.1 0.7 %copy-done.4 = s32[64,16]{0,1:T(8,128)S(1)} copy-done((s32[64,16]{0,1:T(8,128)S(1)}, s32[64,16]{0,1:T(8,128)}, u32[]{:S(2)}) %copy-start.4) | copy-done | bytes 4120
  5.8 0.0 copy-start.5
  5.8 0.7 %copy-done.5 = s32[64]{0:T(128)S(1)} copy-done((s32[64]{0:T(128)S(1)}, s32[64]{0:T(128)}, u32[]{:S(2)}) %copy-start.5) | copy-done | bytes 280
  6.4 0.0 copy-start.6
  6.4 0.7 %copy-done.6 = s32[64]{0:T(128)S(1)} copy-done((s32[64]{0:T(128)S(1)}, s32[64]{0:T(128)}, u32[]{:S(2)}) %copy-start.6) | copy-done | bytes 280
  7.1 34.7 %shard_map.82 = bf16[11,64,384]{2,1,0:T(8,128)(2,1)S(1)} custom-call(bf16[11,64,384]{2,1,0:T(8,128)(2,1)S(1)} %bitcast.8, s32[16,64]{1,0:T(8,128)S(1)} %bitcast.10, s32[16,64]{1,0:T(8,128)S(1)} %bitcast.11, s32[1,64]{1,0:T(1,128)S(1)} %bitcast.12, s32[1,64]{1,0:T(1,128)S(1)} %bitcast.13, bf16[36,16,64]{2,1,0:T(8,128)(2,1)S(1)} %bitcast.9, ...), custom_call_target="tpu_custom_call" | custom-call | tf_op jit(solution)/shard_map/pallas_call | solution.py:232
  41.8 0.8 %copy.10 = bf16[64,11,384]{2,0,1:T(8,128)(2,1)} copy(bf16[64,11,384]{2,0,1:T(8,128)(2,1)S(1)} %bitcast.7) | data formatting | bytes 1081344
Async XLA Ops:
  0.7 1.7 %copy-start = (bf16[3456,384]{1,0:T(8,128)(2,1)S(1)}, bf16[3456,384]{1,0:T(8,128)(2,1)}, u32[]{:S(2)}) copy-start(bf16[3456,384]{1,0:T(8,128)(2,1)} %mix_ref.1) | copy-start | bytes 7962628
  2.4 1.0 %copy-start.1 = (bf16[64,11,384]{2,0,1:T(8,128)(2,1)S(1)}, bf16[64,11,384]{2,0,1:T(8,128)(2,1)}, u32[]{:S(2)}) copy-start(bf16[64,11,384]{2,0,1:T(8,128)(2,1)} %param.8) | copy-start | bytes 1622020
  3.5 0.9 %copy-start.2 = (bf16[64,16,36]{0,1,2:T(8,128)(2,1)S(1)}, bf16[64,16,36]{0,1,2:T(8,128)(2,1)}, u32[]{:S(2)}) copy-start(bf16[64,16,36]{0,1,2:T(8,128)(2,1)} %param.13) | copy-start | bytes 221188
  4.4 0.7 %copy-start.3 = (s32[64,16]{0,1:T(8,128)S(1)}, s32[64,16]{0,1:T(8,128)}, u32[]{:S(2)}) copy-start(s32[64,16]{0,1:T(8,128)} %param.10) | copy-start | bytes 12292
  5.1 0.7 %copy-start.4 = (s32[64,16]{0,1:T(8,128)S(1)}, s32[64,16]{0,1:T(8,128)}, u32[]{:S(2)}) copy-start(s32[64,16]{0,1:T(8,128)} %param.11) | copy-start | bytes 12292
  5.8 0.7 %copy-start.5 = (s32[64]{0:T(128)S(1)}, s32[64]{0:T(128)}, u32[]{:S(2)}) copy-start(s32[64]{0:T(128)} %param.9) | copy-start | bytes 772
  6.4 0.7 %copy-start.6 = (s32[64]{0:T(128)S(1)}, s32[64]{0:T(128)}, u32[]{:S(2)}) copy-start(s32[64]{0:T(128)} %param.12) | copy-start | bytes 772

commit v2 on v1

--- a/solution.py
+++ b/solution.py
@@ -19,21 +19,28 @@
 def kernel(
     lon_size,
     x_ref,
+    rows_in,
+    cols_in,
+    reach_in,
+    counts_in,
+    filt_in,
+    mix_ref,
+    bias_in,
+    out_ref,
+    ext,
+    mix,
     rows_ref,
     cols_ref,
     reach_ref,
     counts_ref,
     filt_ref,
-    mix_ref,
     bias_ref,
-    out_ref,
-    ext,
-    mix,
     hot,
     taps,
     near,
     far,
     conv,
+    small_sem,
     own_sem,
     mix_sem,
     pair_send,
@@ -66,6 +73,21 @@
     own_copy.start()
     mix_copy = pltpu.make_async_copy(mix_ref, mix, mix_sem)
     mix_copy.start()
+    small = [
+        pltpu.make_async_copy(source, target, small_sem.at[index])
+        for index, (source, target) in enumerate(
+            (
+                (rows_in, rows_ref),
+                (cols_in, cols_ref),
+                (reach_in, reach_ref),
+                (counts_in, counts_ref),
+                (filt_in, filt_ref),
+                (bias_in, bias_ref),
+            )
+        )
+    ]
+    for copy in small:
+        copy.start()
 
     barrier = pltpu.get_barrier_semaphore()
     for target in ({"lon": partner}, {"lon": ahead}, {"lon": behind}, {"lat": other}):
@@ -77,13 +99,16 @@
     fwd_from = jnp.where(even, here + cols - HALO, here)
     fwd_to = jnp.where(even, cols - HALO, 2 * cols)
 
-    def pair_copy(step):
+    on_first = jnp.where(even, 0, cols - HALO)
+    off_first = jnp.where(even, HALO, 0)
+
+    def pair_copy(step, which, column, count):
         first = chunk_at(step) * ROWS
         return pltpu.make_async_remote_copy(
-            src_ref=x_ref.at[:, rows_at(first), :],
-            dst_ref=ext.at[pl.ds(there, cols), rows_at(first + ROWS), :],
-            send_sem=pair_send.at[step],
-            recv_sem=pair_recv.at[step],
+            src_ref=x_ref.at[pl.ds(column, count), rows_at(first), :],
+            dst_ref=ext.at[pl.ds(there + column, count), rows_at(first + ROWS), :],
+            send_sem=pair_send.at[which, step],
+            recv_sem=pair_recv.at[which, step],
             device_id={"lon": partner},
             device_id_type=MESH,
         )
@@ -120,9 +145,10 @@
         2, ext.at[pl.ds(fwd_to, HALO), rows_at(edge + ROWS), :], fwd_to, HALO, edge
     )
 
-    pairs = [pair_copy(step) for step in range(chunks)]
+    pairs = [pair_copy(step, 0, on_first, HALO) for step in range(chunks)]
+    rests = [pair_copy(step, 1, off_first, cols - HALO) for step in range(chunks)]
     fwds = [fwd_copy(step) for step in range(chunks)]
-    for copy in pairs:
+    for copy in pairs + rests:
         copy.start()
     lat_own.start()
 
@@ -136,9 +162,11 @@
         same = same_col & ((lane & 15) == (((at & 7) + row - RAD) & 15))
         hot[row] = jnp.where(same, 1.0, 0.0).astype(jnp.bfloat16)
 
+    for copy in small:
+        copy.wait()
     slot = lax.broadcasted_iota(jnp.int32, (SLOTS, rows), 0)
-    code = (cols_ref[...] - reach_ref[...] + 2) * 8 + rows_ref[...]
-    code = jnp.where(slot < counts_ref[...], code, -1)
+    code = (cols_ref[...] - reach_ref[...][None, :] + 2) * 8 + rows_ref[...]
+    code = jnp.where(slot < counts_ref[...][None, :], code, -1)
     place = lax.broadcasted_iota(jnp.int32, (32, rows), 0)
     row_of = lax.broadcasted_iota(jnp.int32, (rows, 256), 0)
     lane_of = lax.broadcasted_iota(jnp.int32, (rows, 256), 1)
@@ -200,25 +228,26 @@
                 conv[col * ROWS : (col + 1) * ROWS, k * width : (k + 1) * width] = both.astype(
                     jnp.bfloat16
                 )
-        pre = jnp.dot(conv[...], mix[...], preferred_element_type=jnp.float32) + bias_ref[...]
+        pre = jnp.dot(conv[...], mix[...], preferred_element_type=jnp.float32) + bias_ref[...][None, :]
         act = pre * (1.0 + lax.erf(pre * (0.5**0.5))) * 0.5
         out_ref[:, pl.ds(first, ROWS), :] = act.astype(jnp.bfloat16).reshape(cols, ROWS, width)
 
     for step in range(chunks):
         pairs[step].wait_recv()
         fwds[step].start()
-        if step == 0:
-            lat_pair.start()
-            lat_own.wait_recv()
+        if step == 1:
             fwds[0].wait_recv()
             lat_fwd.start()
-            lat_pair.wait_recv()
-            lat_fwd.wait_recv()
-        else:
-            fwds[step].wait_recv()
-            compute(step - 1)
+    rests[0].wait_recv()
+    lat_pair.start()
+    for copy in (lat_own, lat_pair, lat_fwd):
+        copy.wait_recv()
+    for step in range(1, chunks):
+        rests[step].wait_recv()
+        fwds[step].wait_recv()
+        compute(step - 1)
     compute(chunks - 1)
-    for copy in pairs + fwds + [lat_own, lat_pair, lat_fwd]:
+    for copy in pairs + rests + fwds + [lat_own, lat_pair, lat_fwd]:
         copy.wait_send()
 
 
@@ -232,37 +261,44 @@
     out = pl.pallas_call(
         functools.partial(kernel, lon_size),
         out_shape=jax.ShapeDtypeStruct((cols, rows, width), jnp.bfloat16),
-        in_specs=[anywhere, vmem, vmem, vmem, vmem, vmem, anywhere, vmem],
+        in_specs=[anywhere] * 8,
         out_specs=vmem,
         scratch_shapes=[
             pltpu.VMEM((3 * cols, rows + 2 * ROWS, width), jnp.bfloat16),
             pltpu.VMEM(mixing.shape, jnp.bfloat16),
+            pltpu.VMEM((SLOTS, rows), jnp.int32),
+            pltpu.VMEM((SLOTS, rows), jnp.int32),
+            pltpu.VMEM((rows,), jnp.int32),
+            pltpu.VMEM((rows,), jnp.int32),
+            pltpu.VMEM((BASIS * BLOCK, SLOTS, rows), jnp.bfloat16),
+            pltpu.VMEM((width,), jnp.float32),
             pltpu.VMEM((8, 128, 256), jnp.bfloat16),
             pltpu.VMEM((BASIS, rows, 256), jnp.float32),
             pltpu.VMEM((span, ROWS, width), jnp.bfloat16),
             pltpu.VMEM((span, ROWS, width), jnp.bfloat16),
             pltpu.VMEM((cols * ROWS, BASIS * width), jnp.bfloat16),
+            dma((6,)),
             dma,
             dma,
-            dma((chunks,)),
-            dma((chunks,)),
+            dma((2, chunks)),
+            dma((2, chunks)),
             dma((chunks,)),
             dma((chunks,)),
             dma((3,)),
             dma((3,)),
         ],
         compiler_params=pltpu.CompilerParams(
-            collective_id=0, has_side_effects=True, vmem_limit_bytes=48 * 2**20
+            collective_id=0, has_side_effects=True, vmem_limit_bytes=60 * 2**20
         ),
     )(
         field.transpose(1, 0, 2),
         slot_rows.T,
         slot_cols.T,
-        reach[None, :],
-        counts[None, :],
+        reach,
+        counts,
         filters.transpose(2, 1, 0),
         mixing,
-        bias[None, :],
+        bias,
     )
     return out.transpose(1, 0, 2)
 

time: 42.9 us -> 28.1 us (0.66)
  the two profiles are of different devices: /device:TPU:0 before, /device:TPU:1 now
where the time goes in v2:
time: 28.1 us; the launch traced here: 28 us
  Pallas kernels  26 us (93%)
  local copies, waits for them, and re-layouts  1.9 us (7%)
    pallas_call x1, Pallas kernels, body(): pl.pallas_call(functools.partial(kernel, lon_size), out_shape=jax.ShapeDt...  26 us
    unnamed x1, local copies, waits for them, and re-layouts  1.9 us

profile of v2, /device:TPU:1, one launch (start us, length us, event | category | flops | bytes accessed | tf_op | source)
XLA Modules:
  0.0 28.0 jit_solution(16586927293063926480)
XLA Ops:
  0.0 26.0 %shard_map.82 = bf16[11,64,384]{2,1,0:T(8,128)(2,1)} custom-call(bf16[11,64,384]{2,1,0:T(8,128)(2,1)} %bitcast.6, s32[16,64]{1,0:T(8,128)} %bitcast.8, s32[16,64]{1,0:T(8,128)} %bitcast.9, s32[64]{0:T(128)} %reach_in.1, s32[64]{0:T(128)} %counts_in.1, bf16[36,16,64]{2,1,0:T(8,128)(2,1)} %bitcast.7, bf16[3456,384]{1,0:T(8,128)(2,1)} %mix_ref.1, f32[384]{0:T(512)} %bias_in.1), custom_call_target="tpu_custom_call" | custom-call | tf_op jit(solution)/shard_map/pallas_call | solution.py:261
  26.0 1.9 %copy.10 = bf16[64,11,384]{2,0,1:T(8,128)(2,1)} copy(bf16[64,11,384]{2,0,1:T(8,128)(2,1)} %bitcast.5) | data formatting | bytes 1081344

commit v3 on v2

--- a/solution.py
+++ b/solution.py
@@ -67,6 +67,10 @@
     def rows_at(start):
         return pl.ds(pl.multiple_of(start, ROWS), ROWS)
 
+    barrier = pltpu.get_barrier_semaphore()
+    for target in ({"lon": partner}, {"lon": ahead}, {"lon": behind}, {"lat": other}):
+        pl.semaphore_signal(barrier, inc=1, device_id=target, device_id_type=MESH)
+
     own_copy = pltpu.make_async_copy(
         x_ref, ext.at[pl.ds(cols, cols), pl.ds(ROWS, rows), :], own_sem
     )
@@ -89,9 +93,6 @@
     for copy in small:
         copy.start()
 
-    barrier = pltpu.get_barrier_semaphore()
-    for target in ({"lon": partner}, {"lon": ahead}, {"lon": behind}, {"lat": other}):
-        pl.semaphore_signal(barrier, inc=1, device_id=target, device_id_type=MESH)
     pl.semaphore_wait(barrier, 4)
 
     there = jnp.where(even, 0, 2 * cols)
@@ -235,7 +236,7 @@
     for step in range(chunks):
         pairs[step].wait_recv()
         fwds[step].start()
-        if step == 1:
+        if step == 2:
             fwds[0].wait_recv()
             lat_fwd.start()
     rests[0].wait_recv()

time: 28.1 us -> 28.1 us (level)
  no operation moved by 1% of the time
where the time goes in v3:
time: 28.1 us; the launch traced here: 27.9 us
  Pallas kernels  26 us (93%)
  local copies, waits for them, and re-layouts  1.9 us (7%)
    pallas_call x1, Pallas kernels, body(): pl.pallas_call(functools.partial(kernel, lon_size), out_shape=jax.ShapeDt...  26 us
    unnamed x1, local copies, waits for them, and re-layouts  1.9 us

profile of v3, /device:TPU:1, one launch (start us, length us, event | category | flops | bytes accessed | tf_op | source)
XLA Modules:
  0.0 27.9 jit_solution(7902878762685540419)
XLA Ops:
  0.0 26.0 %shard_map.82 = bf16[11,64,384]{2,1,0:T(8,128)(2,1)} custom-call(bf16[11,64,384]{2,1,0:T(8,128)(2,1)} %bitcast.6, s32[16,64]{1,0:T(8,128)} %bitcast.8, s32[16,64]{1,0:T(8,128)} %bitcast.9, s32[64]{0:T(128)} %reach_in.1, s32[64]{0:T(128)} %counts_in.1, bf16[36,16,64]{2,1,0:T(8,128)(2,1)} %bitcast.7, bf16[3456,384]{1,0:T(8,128)(2,1)} %mix_ref.1, f32[384]{0:T(512)} %bias_in.1), custom_call_target="tpu_custom_call" | custom-call | tf_op jit(solution)/shard_map/pallas_call | solution.py:262
  26.0 1.9 %copy.10 = bf16[64,11,384]{2,0,1:T(8,128)(2,1)} copy(bf16[64,11,384]{2,0,1:T(8,128)(2,1)} %bitcast.5) | data formatting | bytes 1081344
